TPU v7x, 32 devices: a whole 2x2x4 slice. The times are simulated.
32 devices in a mesh: tm: 2 (over y), rows: 16 (over z, x, core).
Axes of the slice: x: 2, y: 2, z: 4, core: 2. Of those that a mesh axis runs over, the one named last changes fastest.
Arguments:
- inputs: bfloat16 [4, 64, 16, 256], P('tm', 'rows'), may hold values from -6 to 6
- cotangent: bfloat16 [4, 64, 16, 256], P('tm', 'rows'), may hold values from -6 to 6
- kernel: bfloat16 [27, 256, 256], P(None, 'rows', 'tm'), may hold values from -0.078125 to 0.078125
Outputs:
- grad_inputs: bfloat16 [4, 64, 16, 256], P('tm', 'rows')
- grad_kernel: float32 [27, 256, 256], P(None, 'rows', 'tm')
All inputs are finite; a program needn't handle non-finite values.
Results may differ from a plain program's by a relative error of at most 0.003.
Values may be sent and summed in bfloat16 or wider, within the bound.
A program may use at most 64 MiB of HBM per device.

v0:
```python
import functools

import jax
import jax.numpy as jnp
from jax import lax
from jax.experimental import pallas as pl
from jax.experimental.pallas import tpu as pltpu
from jax.sharding import PartitionSpec as P

MESH = pl.DeviceIdType.MESH
LANES = 128


def extended(block, sides, width):
    for axis, dim in sides:
        count = lax.axis_size(axis)
        forward = [(i, i + 1) for i in range(count - 1)]
        backward = [(target, source) for source, target in forward]
        low = lax.ppermute(
            lax.slice_in_dim(block, block.shape[dim] - width, None, axis=dim), axis, forward
        )
        high = lax.ppermute(lax.slice_in_dim(block, 0, width, axis=dim), axis, backward)
        block = jnp.concatenate([low, block, high], axis=dim)
    return block


def silu_slope(values):
    logistic = jax.nn.sigmoid(values)
    return logistic * (1.0 + values * (1.0 - logistic))


def widen_cols(values):
    return jnp.pad(values, ((0, 0), (0, 0), (1, 1), (0, 0)))


def tap_columns(padded, frames, height, across):
    pieces = []
    for time_tap in range(3):
        for row_tap in range(3):
            for col_tap in range(3):
                start_time, start_row, start_col = (2 - time_tap, 2 - row_tap, 2 - col_tap)
                pieces.append(
                    padded[
                        start_time : start_time + frames,
                        start_row : start_row + height,
                        start_col : start_col + across,
                    ]
                )
    stacked = jnp.stack(pieces, 3)
    return stacked.reshape(frames * height * across, 27, padded.shape[3])


def backward_piece(columns, portion):
    return lax.dot_general(
        columns, portion, (((1, 2), (0, 2)), ((), ())), preferred_element_type=jnp.float32
    )


def kernel_grad(haloed, gradient, factor):
    height = gradient.shape[1]
    across = gradient.shape[2]
    channels = haloed.shape[3]
    split_grads = lax.all_to_all(gradient, "tm", split_axis=3, concat_axis=0, tiled=True)
    width_out = split_grads.shape[3]
    padded_grads = jnp.pad(split_grads, ((0, 2), (0, 0), (0, 0), (0, 0)))
    portion = lax.all_gather(haloed, "tm", axis=0, tiled=True)
    offset = jnp.int32(0)
    portion_frames = portion.shape[0]
    widened = widen_cols(portion)
    spatial = jnp.stack(
        [
            widened[:, row_tap : row_tap + height, col_tap : col_tap + across]
            for row_tap in range(3)
            for col_tap in range(3)
        ],
        3,
    )
    shifted_grads = jnp.stack(
        [
            lax.dynamic_slice_in_dim(padded_grads, offset + 2 - time_tap, portion_frames, 0)
            for time_tap in range(3)
        ],
        0,
    )
    contribution = lax.dot_general(
        spatial,
        shifted_grads,
        (((0, 1, 2), (1, 2, 3)), ((), ())),
        preferred_element_type=jnp.float32,
    )
    contribution = jnp.transpose(contribution, (2, 0, 1, 3)).reshape(27, channels, width_out)
    return lax.psum_scatter(contribution * factor, "rows", scatter_dimension=1, tiled=True)


def gathered_plan(inputs, cotangent, kernel):
    frames, height, across, channels = inputs.shape
    positions = frames * height * across
    rows_kernel = lax.all_gather(kernel, "rows", axis=1, tiled=True)
    act = jax.nn.silu(inputs.astype(jnp.float32)).astype(jnp.bfloat16)
    paired = jnp.concatenate([act, cotangent], 3)
    paired_rows = extended(paired, (("rows", 1),), 1)
    halo_act = paired_rows[:, :, :, :channels]
    halo_grad = paired_rows[:, :, :, channels:]
    split_bands = lax.all_to_all(halo_grad, "tm", split_axis=3, concat_axis=0, tiled=True)
    total_frames = split_bands.shape[0]
    padded_bands = jnp.pad(split_bands, ((0, 2), (0, 0), (0, 0), (0, 0)))
    cols_all = tap_columns(widen_cols(padded_bands), total_frames, height, across)
    partial_terms = backward_piece(cols_all, rows_kernel).reshape(
        total_frames // frames, positions, channels
    )
    grad_act = lax.psum_scatter(partial_terms, "tm", scatter_dimension=0, tiled=True)
    grad_act = grad_act.reshape(frames, height, across, channels)
    grad_inputs = (
        cotangent.astype(jnp.float32) + grad_act * silu_slope(inputs.astype(jnp.float32))
    ).astype(jnp.bfloat16)
    factor = float(frames * lax.axis_size("tm") * height * lax.axis_size("rows") * across) ** (-0.5)
    grad_kernel = kernel_grad(halo_act, cotangent, factor)
    return (grad_inputs, grad_kernel)


def exchange_fits(inputs, cotangent, kernel):
    frames, height, across, channels = inputs.shape
    groups, bands = lax.axis_size("tm"), lax.axis_size("rows")
    own_in, own_out = kernel.shape[1], kernel.shape[2]
    return (
        frames == 2
        and frames * height * across == LANES
        and across == 16
        and own_in == 16
        and own_out == LANES
        and groups == 2
        and bands == 16
        and channels == own_in * bands == own_out * groups
        and frames * groups * height * bands * across * own_out * 2 <= 4 * 2**20
    )


def exchange_kernel(
    groups, bands, factor,
    inputs_hbm, cot_hbm, kernel_hbm, grad_in_ref, grad_kernel_ref,
    inputs_ref, cot_ref, taps_ref, turned, grads, acts, act_edge, act_send, sums, part_send, part,
    back_send, back, spatial, share, share_in,
    load_sem, line_recv, side_recv, edge_recv, taps_recv, line_send, side_send, edge_send, taps_send,
    act_send_sem, act_recv_sem, act_edge_send, act_edge_recv, cross_send_sem, cross_recv_sem,
    part_send_sem, part_recv_sem, back_send_sem, back_recv_sem, share_send, share_recv,
):
    frames, height, across, channels = inputs_ref.shape
    own_in = grad_kernel_ref.shape[1]
    pair_in = 2 * own_in
    positions = frames * height * across
    chips = bands // 2
    depth = chips // 2
    near = bands // 2
    rows = height * near
    plane = rows * across
    all_frames = frames * groups
    half = LANES // 2

    group, band = lax.axis_index("tm"), lax.axis_index("rows")
    partner = (group + 1) % groups
    chip, core = band // 2, band % 2
    layer, column = chip // 2, chip % 2
    keeper = layer // 2
    at_home = keeper == core
    other_core = (group, chip * 2 + 1 - core)

    def device_of(layer_of, column_of, core_of):
        return (layer_of * 2 + column_of) * 2 + core_of

    def region(group_of, near_band):
        return grads.at[pl.ds(group_of * frames, frames), pl.ds(1 + near_band * height, height)]

    def wait_bytes(ref, sem):
        pltpu.make_async_copy(ref, ref, sem).wait()

    def remote(source, target, send_sem, recv_sem, device):
        return pltpu.make_async_remote_copy(
            src_ref=source, dst_ref=target, send_sem=send_sem, recv_sem=recv_sem,
            device_id=device, device_id_type=MESH,
        )

    load_inputs = pltpu.make_async_copy(inputs_hbm, inputs_ref, load_sem.at[0])
    load_cot = pltpu.make_async_copy(cot_hbm, cot_ref, load_sem.at[1])
    load_kernel = pltpu.make_async_copy(kernel_hbm, taps_ref.at[core], load_sem.at[2])
    load_inputs.start()
    load_cot.start()
    load_kernel.start()

    barrier = pltpu.get_barrier_semaphore()

    def greet(step, carry):
        pl.semaphore_signal(
            barrier, inc=1, device_id=(group, (band + step) % bands), device_id_type=MESH
        )
        return carry

    def greet_column(step, carry):
        pl.semaphore_signal(
            barrier, inc=1, device_id=(partner, device_of(step // 2, column, step % 2)),
            device_id_type=MESH,
        )
        return carry

    lax.fori_loop(1, bands, greet, 0)
    lax.fori_loop(0, 2 * depth, greet_column, 0)
    pl.semaphore_wait(barrier, bands - 1 + 2 * depth)

    own_part = cot_hbm.at[:, :, :, pl.ds(pl.multiple_of(group * LANES, LANES), LANES)]
    other_part = cot_hbm.at[:, :, :, pl.ds(pl.multiple_of(partner * LANES, LANES), LANES)]
    landing = region(group, band % near)

    def send_line(turn, carry):
        layer_of = (layer // 2 + turn // 2) % 2 * 2 + (layer + turn) % 2
        target = device_of(layer_of, column, keeper)
        arrival = line_recv.at[layer % 2, core]

        @pl.when(target == band)
        def _():
            pltpu.make_async_copy(own_part, landing, arrival.at[0]).start()

        @pl.when(target != band)
        def _():
            remote(own_part, landing, line_send, arrival.at[0], (group, target)).start()

        remote(other_part, landing, line_send, arrival.at[1], (partner, target)).start()
        return carry

    lax.fori_loop(0, depth, send_line, 0)
    load_kernel.wait()
    remote(taps_ref.at[core], taps_ref.at[core], taps_send, taps_recv, other_core).start()

    load_inputs.wait()
    values = inputs_ref[...].reshape(positions, channels).astype(jnp.float32)
    act = values * jax.nn.sigmoid(values)
    act_send[...] = act.T.astype(jnp.bfloat16).reshape(chips, pair_in, positions)

    def send_act(step, carry):
        to_chip = (chip + step) % chips
        target = to_chip * 2 + keeper
        source, place = act_send.at[to_chip], acts.at[group, band % near]

        @pl.when(target == band)
        def _():
            pltpu.make_async_copy(source, place, act_recv_sem).start()

        @pl.when(target != band)
        def _():
            remote(source, place, act_send_sem, act_recv_sem, (group, target)).start()

        return carry

    lax.fori_loop(0, chips, send_act, 0)

    lane = lax.broadcasted_iota(jnp.int32, (pair_in, plane), 1)
    col = lane % across
    low = lax.broadcasted_iota(jnp.int32, (pair_in, LANES), 1) < half

    def moved(block, by_col):
        if by_col == 0:
            return block
        cells = col[:, : block.shape[1]] + by_col
        block = pltpu.roll(block, (-by_col) % block.shape[1], 1)
        return jnp.where((cells >= 0) & (cells < across), block, 0.0)

    wait_bytes(taps_ref.at[1 - core], taps_recv)
    wide = 3 * own_in
    for time_tap in range(3):
        for row_tap in range(3):
            at = pl.ds(9 * time_tap + 3 * row_tap, 3)
            block = jnp.concatenate(
                [taps_ref[0, at].reshape(wide, LANES), taps_ref[1, at].reshape(wide, LANES)]
            ).astype(jnp.float32)
            block = jnp.concatenate([block, jnp.zeros((LANES - 2 * wide, LANES), jnp.float32)])
            turned[pl.ds(time_tap * LANES, LANES), pl.ds(row_tap * LANES, LANES)] = (
                block.T.astype(jnp.bfloat16)
            )
    spatial[pl.ds(0, 2)] = jnp.zeros((2,) + spatial.shape[1:], spatial.dtype)
    grads[:, pl.ds((rows + 1) * core, 1)] = jnp.zeros((all_frames, 1, across, LANES), jnp.bfloat16)

    def sum_rows(first, count):
        cells = [
            grads[frame, pl.ds(first, count)].reshape(count * across, LANES)
            for frame in range(all_frames)
        ] + [jnp.zeros((count * across, LANES), jnp.bfloat16)] * 2
        windows = jnp.concatenate(
            [
                jnp.concatenate([cells[frame + 2 - tap] for tap in range(3)], axis=1)
                for frame in range(all_frames)
            ],
            axis=0,
        )
        result = lax.dot_general(
            windows, turned[...], (((1,), (0,)), ((), ())), preferred_element_type=jnp.float32
        ).reshape(all_frames, count * across, 3 * LANES)
        start = first * across
        if not isinstance(start, int):
            start = pl.multiple_of(start, across)
        for row_tap in range(3):
            sums[row_tap, :, pl.ds(start, count * across)] = result[
                :, :, row_tap * LANES : (row_tap + 1) * LANES
            ]

    def all_of(near_band):
        return grads.at[:, pl.ds(1 + near_band * height, height)]

    edge_from = grads.at[:, pl.ds((1 - core) * rows + core, 1)]
    edge_to = grads.at[:, pl.ds(core * (rows + 1), 1)]
    edge_in = grads.at[:, pl.ds((1 - core) * (rows + 1), 1)]

    def pass_edge(near_band):
        @pl.when(near_band == (1 - core) * (near - 1))
        def _():
            remote(edge_from, edge_to, edge_send, edge_recv, other_core).start()

    def pass_line(turn, carry):
        odd = (layer + turn) % 2
        for core_of in range(2):
            near_band = odd * 4 + column * 2 + core_of
            for piece in range(groups):
                wait_bytes(region((group + piece) % groups, near_band),
                           line_recv.at[odd, core_of, piece])
            remote(
                all_of(near_band), all_of(near_band), side_send, side_recv.at[odd, core_of],
                (group, device_of(layer, 1 - column, core)),
            ).start()
            pass_edge(near_band)
        return carry

    def take_side(turn):
        odd = (layer + turn) % 2
        for core_of in range(2):
            near_band = odd * 4 + (1 - column) * 2 + core_of
            wait_bytes(all_of(near_band), side_recv.at[odd, core_of])
            pass_edge(near_band)

    lax.fori_loop(0, 2, pass_line, 0)

    wait_bytes(acts.at[group], act_recv_sem)
    remote(
        acts.at[group], acts.at[group], cross_send_sem, cross_recv_sem, (partner, band)
    ).start()

    def sum_chips(turn, carry):
        odd = (layer + turn) % 2
        far = turn // 2

        @pl.when(far == 1)
        def _():
            take_side(turn)

        sum_rows(1 + (odd * 2 + column + far - 2 * column * far) * 2 * height, 2 * height)
        return carry

    lax.fori_loop(0, 4, sum_chips, 0)

    wait_bytes(acts.at[partner], cross_recv_sem)
    remote(
        acts.at[:, (1 - core) * (near - 1)], act_edge, act_edge_send, act_edge_recv, other_core
    ).start()
    wait_bytes(edge_in, edge_recv)
    sum_rows(0, 1)
    sum_rows(rows + 1, 1)

    def grad_act_of(frame):
        mixed = None
        for row_tap in range(3):
            term = sums[row_tap, frame, pl.ds(across * (2 - row_tap), plane)]
            mixed = term if mixed is None else mixed + term
        mixed = mixed.T
        result = None
        for col_tap in range(3):
            at = col_tap * own_in
            term = jnp.concatenate([mixed[at : at + own_in], mixed[wide + at : wide + at + own_in]])
            term = moved(term, 1 - col_tap)
            result = term if result is None else result + term
        return result

    def shares(at, carry):
        owner = (partner + at // frames) % groups
        part_send[at] = grad_act_of(owner * frames + at % frames)

        @pl.when(at < frames)
        def _():
            remote(
                part_send.at[at], part.at[at], part_send_sem.at[at], part_recv_sem.at[at],
                (partner, band),
            ).start()

        return carry

    lax.fori_loop(0, all_frames, shares, 0)

    wait_bytes(act_edge, act_edge_recv)

    def shift_acts(group_of, carry):
        edge_tile = act_edge[group_of].astype(jnp.float32)
        above = jnp.where(core == 1, edge_tile, 0.0)
        below = jnp.where(core == 0, edge_tile, 0.0)
        for at in range(frames):
            tiles = []
            for pair in range(near // 2):
                x = acts[group_of, 2 * pair].astype(jnp.float32)
                y = acts[group_of, 2 * pair + 1].astype(jnp.float32)
                if at == 0:
                    tiles.append(jnp.where(low, x, pltpu.roll(y, half, 1)))
                else:
                    tiles.append(jnp.where(low, pltpu.roll(x, half, 1), y))
            whole = jnp.concatenate(tiles, axis=1)
            for col_tap in range(3):
                shifted = moved(whole, col_tap - 1)
                top = pltpu.roll(moved(above, col_tap - 1), (2 * LANES - at * half - 48) % LANES, 1)
                end = pltpu.roll(moved(below, col_tap - 1), (2 * LANES - at * half - across) % LANES, 1)
                repeat = plane // LANES
                top = jnp.concatenate([top] * repeat, axis=1)
                end = jnp.concatenate([end] * repeat, axis=1)
                up = jnp.where(lane < across, top, pltpu.roll(shifted, across, 1))
                down = jnp.where(lane >= plane - across, end, pltpu.roll(shifted, plane - across, 1))
                for row_tap, block in enumerate((up, shifted, down)):
                    tap = 3 * row_tap + col_tap
                    spatial[2 + group_of * frames + at, pl.ds(tap * pair_in, pair_in)] = (
                        block.astype(jnp.bfloat16)
                    )
        return carry

    lax.fori_loop(0, groups, shift_acts, 0)
    share[...] = jnp.zeros_like(share)

    for at in range(frames):
        wait_bytes(part.at[at], part_recv_sem.at[at])
    first, second = [part_send[frames + at] + part[at] for at in range(frames)]
    for pair in range(near // 2):
        x = first[:, pair * LANES : (pair + 1) * LANES]
        y = second[:, pair * LANES : (pair + 1) * LANES]
        back_send[2 * pair] = jnp.where(low, x, pltpu.roll(y, half, 1))
        back_send[2 * pair + 1] = jnp.where(low, pltpu.roll(x, half, 1), y)

    def send_back(step, carry):
        near_band = (band + step) % near
        target = core * near + near_band
        source, place = back_send.at[near_band], back.at[chip]

        @pl.when(target == band)
        def _():
            pltpu.make_async_copy(source, place, back_recv_sem).start()

        @pl.when(target != band)
        def _():
            remote(source, place, back_send_sem, back_recv_sem, (group, target)).start()

        return carry

    lax.fori_loop(0, near, send_back, 0)

    def kernel_taps(frame, carry):
        cells = grads[frame, pl.ds(1, rows)].reshape(plane, LANES)
        for time_tap in range(3):
            term = lax.dot_general(
                spatial[frame + time_tap], cells, (((1,), (0,)), ((), ())),
                preferred_element_type=jnp.float32,
            ).reshape(9, 2, own_in, LANES)
            own = pl.ds(9 * time_tap, 9)
            for core_of in range(2):
                share[core_of, own] = share[core_of, own] + term[:, core_of]
        return carry

    lax.fori_loop(0, all_frames, kernel_taps, 0)
    remote(share.at[1 - core], share_in, share_send, share_recv, other_core).start()

    wait_bytes(back, back_recv_sem)
    grad_act = back[...].reshape(channels, positions).T
    values = inputs_ref[...].reshape(positions, channels).astype(jnp.float32)
    load_cot.wait()
    cot = cot_ref[...].reshape(positions, channels).astype(jnp.float32)
    grad_in = cot + grad_act * silu_slope(values)
    grad_in_ref[...] = grad_in.astype(jnp.bfloat16).reshape(grad_in_ref.shape)
    wait_bytes(share_in, share_recv)
    grad_kernel_ref[...] = (share[core] + share_in[...]) * factor

    sent = 2 * depth

    @pl.when(at_home)
    def _():
        wait_bytes(grads.at[pl.ds(0, frames), pl.ds(0, height * (sent - 1))], line_send)
        wait_bytes(acts.at[0, pl.ds(0, chips - 1)], act_send_sem)
        wait_bytes(back.at[pl.ds(0, near - 1)], back_send_sem)

    @pl.when(jnp.logical_not(at_home))
    def _():
        wait_bytes(grads.at[pl.ds(0, frames), pl.ds(0, height * sent)], line_send)
        wait_bytes(acts.at[0, pl.ds(0, chips)], act_send_sem)
        wait_bytes(back.at[pl.ds(0, near)], back_send_sem)

    wait_bytes(grads.at[:, pl.ds(0, 4 * height)], side_send)
    wait_bytes(edge_from, edge_send)
    wait_bytes(taps_ref.at[core], taps_send)
    wait_bytes(act_edge, act_edge_send)
    wait_bytes(acts.at[group], cross_send_sem)
    for at in range(frames):
        wait_bytes(part_send.at[at], part_send_sem.at[at])
    wait_bytes(share_in, share_send)


def exchange_plan(inputs, cotangent, kernel):
    frames, height, across, channels = inputs.shape
    taps, own_in, own_out = kernel.shape
    groups, bands = lax.axis_size("tm"), lax.axis_size("rows")
    positions = frames * height * across
    all_frames, chips, near = frames * groups, bands // 2, bands // 2
    rows = height * near
    plane = rows * across
    factor = float(all_frames * 2 * plane) ** (-0.5)
    dma = pltpu.SemaphoreType.DMA
    bf16, f32 = jnp.bfloat16, jnp.float32
    return pl.pallas_call(
        functools.partial(exchange_kernel, groups, bands, factor),
        out_shape=(pltpu.VMEM(inputs.shape, bf16), pltpu.VMEM(kernel.shape, f32)),
        in_specs=[pl.BlockSpec(memory_space=pltpu.HBM)] * 3,
        out_specs=[pl.BlockSpec(memory_space=pltpu.VMEM)] * 2,
        scratch_shapes=[
            pltpu.VMEM(inputs.shape, bf16),
            pltpu.VMEM(cotangent.shape, bf16),
            pltpu.VMEM((2,) + kernel.shape, bf16),
            pltpu.VMEM((3 * LANES, 3 * LANES), bf16),
            pltpu.VMEM((all_frames, rows + 2, across, own_out), bf16),
            pltpu.VMEM((groups, near, 2 * own_in, positions), bf16),
            pltpu.VMEM((groups, 2 * own_in, positions), bf16),
            pltpu.VMEM((chips, 2 * own_in, positions), bf16),
            pltpu.VMEM((3, all_frames, plane + 2 * across, LANES), f32),
            pltpu.VMEM((all_frames, 2 * own_in, plane), f32),
            pltpu.VMEM((frames, 2 * own_in, plane), f32),
            pltpu.VMEM((near, 2 * own_in, positions), f32),
            pltpu.VMEM((chips, 2 * own_in, positions), f32),
            pltpu.VMEM((all_frames + 2, 18 * own_in, plane), bf16),
            pltpu.VMEM((2,) + kernel.shape, f32),
            pltpu.VMEM(kernel.shape, f32),
            dma((3,)),
            dma((2, 2, groups)),
            dma((2, 2)),
        ] + [dma] * 12 + [dma((frames,))] * 2 + [dma] * 4,
        compiler_params=pltpu.CompilerParams(
            collective_id=0, has_side_effects=True, vmem_limit_bytes=60 * 2**20
        ),
    )(inputs, cotangent, kernel)


def local(inputs, cotangent, kernel):
    if exchange_fits(inputs, cotangent, kernel):
        return exchange_plan(inputs, cotangent, kernel)
    return gathered_plan(inputs, cotangent, kernel)


def solution(mesh):
    return jax.shard_map(
        local,
        mesh=mesh,
        in_specs=(P("tm", "rows", None, None), P("tm", "rows", None, None), P(None, "rows", "tm")),
        out_specs=(P("tm", "rows", None, None), P(None, "rows", "tm")),
        check_vma=False,
    )
```

profile of v0, /device:TPU:0, one launch (start us, length us, event | category | flops | bytes accessed | tf_op | source)
XLA Modules:
  0.0 32.7 jit_solution(188407215201526362)
XLA Ops:
  0.6 30.8 %shard_map.50 = (bf16[2,4,16,256]{3,2,1,0:T(8,128)(2,1)S(1)}, f32[27,16,128]{2,1,0:T(8,128)S(1)}) custom-call(bf16[2,4,16,256]{3,2,1,0:T(8,128)(2,1)} %inputs_hbm.1, bf16[2,4,16,256]{3,2,1,0:T(8,128)(2,1)} %cot_hbm.1, bf16[27,16,128]{2,1,0:T(8,128)(2,1)} %kernel_hbm.1), custom_call_target="tpu_custom_call" | custom-call | tf_op jit(solution)/shard_map/pallas_call | solution.py:514
  31.4 0.6 %copy.7 = bf16[2,4,16,256]{3,2,1,0:T(8,128)(2,1)} copy(bf16[2,4,16,256]{3,2,1,0:T(8,128)(2,1)S(1)} %get-tuple-element.2) | data formatting | bytes 131072
  32.0 0.7 %copy.8 = f32[27,16,128]{2,1,0:T(8,128)} copy(f32[27,16,128]{2,1,0:T(8,128)S(1)} %get-tuple-element.3) | data formatting | bytes 442368
where the time goes:
time: 32.9 us; the launch traced here: 32.7 us
  Pallas kernels  30.8 us (94%)
  local copies, waits for them, and re-layouts  1.32 us (4%)
  between operations  0.64 us (2%)
    pallas_call x1, Pallas kernels, exchange_plan(): pl.pallas_call(functools.partial(exchange_kernel, groups, bands, factor),...  30.8 us
    unnamed x2, local copies, waits for them, and re-layouts  1.32 us

commit v1 on v0

--- a/solution.py
+++ b/solution.py
@@ -209,7 +209,8 @@
     other_part = cot_hbm.at[:, :, :, pl.ds(pl.multiple_of(partner * LANES, LANES), LANES)]
     landing = region(group, band % near)
 
-    def send_line(turn, carry):
+    def send_line(step, carry):
+        turn = depth - 1 - step
         layer_of = (layer // 2 + turn // 2) % 2 * 2 + (layer + turn) % 2
         target = device_of(layer_of, column, keeper)
         arrival = line_recv.at[layer % 2, core]

time: 32.9 us -> 33.5 us (1.018)
  Pallas kernels: 30.8 us -> 31.4 us
    pallas_call x1, Pallas kernels: 30.8 us -> 31.4 us  [exchange_plan(): pl.pallas_call(functools.partial(exchange_kernel, groups, bands, factor),...]
where the time goes in v1:
time: 33.5 us; the launch traced here: 33.4 us
  Pallas kernels  31.4 us (94%)
  local copies, waits for them, and re-layouts  1.32 us (4%)
  between operations  0.64 us (2%)
    pallas_call x1, Pallas kernels, exchange_plan(): pl.pallas_call(functools.partial(exchange_kernel, groups, bands, factor),...  31.4 us
    unnamed x2, local copies, waits for them, and re-layouts  1.32 us

profile of v1, /device:TPU:0, one launch (start us, length us, event | category | flops | bytes accessed | tf_op | source)
XLA Modules:
  0.0 33.4 jit_solution(17649959852182423387)
XLA Ops:
  0.6 31.4 %shard_map.50 = (bf16[2,4,16,256]{3,2,1,0:T(8,128)(2,1)S(1)}, f32[27,16,128]{2,1,0:T(8,128)S(1)}) custom-call(bf16[2,4,16,256]{3,2,1,0:T(8,128)(2,1)} %inputs_hbm.1, bf16[2,4,16,256]{3,2,1,0:T(8,128)(2,1)} %cot_hbm.1, bf16[27,16,128]{2,1,0:T(8,128)(2,1)} %kernel_hbm.1), custom_call_target="tpu_custom_call" | custom-call | tf_op jit(solution)/shard_map/pallas_call | solution.py:515
  32.0 0.6 %copy.7 = bf16[2,4,16,256]{3,2,1,0:T(8,128)(2,1)} copy(bf16[2,4,16,256]{3,2,1,0:T(8,128)(2,1)S(1)} %get-tuple-element.2) | data formatting | bytes 131072
  32.7 0.7 %copy.8 = f32[27,16,128]{2,1,0:T(8,128)} copy(f32[27,16,128]{2,1,0:T(8,128)S(1)} %get-tuple-element.3) | data formatting | bytes 442368
